TPU v7x, 512 devices: a whole 4x8x8 slice. The times are simulated.
512 devices in a mesh: seq: 128 (over z_lo, y, x), head: 4 (over z_hi, core).
Axes of the slice: x: 4, y: 8, z: 8 (z_hi: 2, z_lo: 4; z = z_hi * 4 + z_lo), core: 2. Of those that a mesh axis runs over, the one named last changes fastest.
Arguments:
- query_rows: bfloat16 [49152, 1536], P(('seq', 'head')), may hold values from -6 to 6
- key_rows: bfloat16 [49152, 1536], P(('seq', 'head')), may hold values from -6 to 6
- value_rows: bfloat16 [49152, 1536], P(('seq', 'head')), may hold values from -6 to 6
- cotangent: bfloat16 [49152, 1536], P(('seq', 'head')), may hold values from -6 to 6
- neighbours: int32 [128, 3], replicated, may hold values from -1 to 127, as said below
Outputs:
- attended: bfloat16 [49152, 1536], P(('seq', 'head'))
- query_grad: bfloat16 [49152, 1536], P(('seq', 'head'))
- key_grad: bfloat16 [49152, 1536], P(('seq', 'head'))
- value_grad: bfloat16 [49152, 1536], P(('seq', 'head'))
Inputs may be any that keep to these rules, and one draw needn't show every extreme that they name: `neighbours`: tiles lie on a grid of 2 time steps, each of 64 tiles in rows of 4, in time-major order: tile t is at time t // 64 and column t % 4. Row t starts with t itself; its other entries are distinct tiles u of the same row of the same time step or of the same row position at a time step one away, whose column differs from t's by at most 1, in any order, or -1 for an unused slot; the number of used slots differs from tile to tile.
All inputs are finite; a program needn't handle non-finite values.
Results may differ from a plain program's by a relative error of at most 0.0065.
The roundings to bfloat16 on the way count: a program that leaves them out, or rounds other values in their place, can miss the bound.
Values may be sent and summed in bfloat16 or wider, within the bound.
A program may use at most 64 MiB of HBM per device.

v0:
```python
import math

import jax
import jax.numpy as jnp
from jax import lax
from jax.sharding import PartitionSpec as P

HD = 128
TILE = 384


def shifted(array, axis, by):
    peers = lax.axis_size(axis)
    pairs = [(i, i + by) for i in range(peers) if 0 <= i + by < peers]
    return lax.ppermute(array, axis, pairs)


def head_scores(head_queries, head_keys, live_slots, score_scale):
    raw_scores = (
        jnp.einsum("id,njd->inj", head_queries, head_keys, preferred_element_type=jnp.float32)
        * score_scale
    )
    return jnp.where(live_slots[None, :, None], raw_scores, -1e30)


def head_forward(head_queries, head_keys, head_values, live_slots, score_scale):
    masked = head_scores(head_queries, head_keys, live_slots, score_scale)
    row_top = jnp.max(masked, axis=(1, 2), keepdims=True)
    row_total = jnp.sum(jnp.exp(masked - row_top), axis=(1, 2), keepdims=True)
    log_norm = row_top + jnp.log(row_total)
    probs_low = jnp.exp(masked - log_norm).astype(jnp.bfloat16)
    attended = jnp.einsum(
        "inj,njd->id", probs_low, head_values, preferred_element_type=jnp.float32
    ).astype(jnp.bfloat16)
    return (attended, log_norm[:, 0, 0])


def head_backward(
    head_queries, head_cot, head_keys, head_values, live_slots, log_norm, row_delta, score_scale
):
    masked = head_scores(head_queries, head_keys, live_slots, score_scale)
    prob_full = jnp.exp(masked - log_norm[:, None, None])
    prob_grad = jnp.einsum("id,njd->inj", head_cot, head_values, preferred_element_type=jnp.float32)
    dscore_low = (prob_full * (prob_grad - row_delta[:, None, None]) * score_scale).astype(
        jnp.bfloat16
    )
    results = ()
    results = results + (
        jnp.einsum("inj,njd->id", dscore_low, head_keys, preferred_element_type=jnp.float32).astype(
            jnp.bfloat16
        ),
    )
    probs_low = prob_full.astype(jnp.bfloat16)
    key_part = jnp.einsum(
        "inj,id->njd", dscore_low, head_queries, preferred_element_type=jnp.float32
    )
    value_part = jnp.einsum("inj,id->njd", probs_low, head_cot, preferred_element_type=jnp.float32)
    results = results + (key_part, value_part)
    return results


def tile_forward(tile_queries, near_keys, near_values, live_slots, score_scale):

    def one_head(inputs):
        return head_forward(inputs[0], inputs[1], inputs[2], live_slots, score_scale)

    attended, log_norm = lax.map(
        one_head,
        (
            tile_queries.transpose(1, 0, 2),
            near_keys.transpose(2, 0, 1, 3),
            near_values.transpose(2, 0, 1, 3),
        ),
    )
    return (attended.transpose(1, 0, 2), log_norm)


def tile_backward(
    tile_queries, tile_cot, near_keys, near_values, live_slots, log_norm, row_delta, score_scale
):

    def one_head(inputs):
        return head_backward(
            inputs[0],
            inputs[1],
            inputs[2],
            inputs[3],
            live_slots,
            inputs[4],
            inputs[5],
            score_scale,
        )

    mapped = lax.map(
        one_head,
        (
            tile_queries.transpose(1, 0, 2),
            tile_cot.transpose(1, 0, 2),
            near_keys.transpose(2, 0, 1, 3),
            near_values.transpose(2, 0, 1, 3),
            log_norm,
            row_delta,
        ),
    )
    results = ()
    position = 0
    results = results + (mapped[0].transpose(1, 0, 2),)
    position = 1
    results = results + (
        mapped[position].transpose(1, 2, 0, 3),
        mapped[position + 1].transpose(1, 2, 0, 3),
    )
    return results


def on_device(query_rows, key_rows, value_rows, cotangent, neighbours):
    query_local, key_local, value_local, cot_local = (
        lax.all_to_all(query_rows, "head", split_axis=1, concat_axis=0, tiled=True),
        lax.all_to_all(key_rows, "head", split_axis=1, concat_axis=0, tiled=True),
        lax.all_to_all(value_rows, "head", split_axis=1, concat_axis=0, tiled=True),
        lax.all_to_all(cotangent, "head", split_axis=1, concat_axis=0, tiled=True),
    )
    row_count, feat_count = query_local.shape
    tiles_here = row_count // TILE
    heads_here = feat_count // HD
    slot_count = neighbours.shape[1]
    axis_count = lax.axis_size("seq")
    half_axis = axis_count // 2
    dev_offsets = [sign * half_axis + step for sign in (-1, 0, 1) for step in (-1, 0, 1)]
    block_total = len(dev_offsets)
    offset_table = jnp.array(dev_offsets, dtype=jnp.int32)
    block_numbers = jnp.arange(block_total, dtype=jnp.int32)
    window_tiles = block_total * tiles_here
    score_scale = 1.0 / math.sqrt(HD)
    own_index = lax.axis_index("seq")
    first_tile = own_index * tiles_here
    own_list = lax.dynamic_slice_in_dim(neighbours, first_tile, tiles_here, 0)
    live_slots = own_list >= 0
    safe_ids = jnp.where(live_slots, own_list, 0)
    dev_delta = safe_ids // tiles_here - own_index
    block_of = jnp.sum(
        block_numbers * (dev_delta[..., None] == offset_table).astype(jnp.int32), axis=-1
    )
    slot_ids = jnp.where(live_slots, block_of * tiles_here + safe_ids % tiles_here, 0)
    kv_pair = jnp.stack((key_local, value_local))
    pieces = []
    for offset in dev_offsets:
        if offset == 0:
            pieces.append(kv_pair)
        else:
            pieces.append(shifted(kv_pair, "seq", -offset))
    window_flat = jnp.stack(pieces, axis=1)
    window = window_flat.reshape(2, window_tiles, TILE, heads_here, HD)
    query_tiles = query_local.reshape(tiles_here, TILE, heads_here, HD)
    cot_tiles = cot_local.reshape(tiles_here, TILE, heads_here, HD)

    def forward_one(inputs):
        tile_queries, tile_slots, tile_live = inputs
        near_keys = jnp.take(window[0], tile_slots, axis=0)
        near_values = jnp.take(window[1], tile_slots, axis=0)
        return tile_forward(tile_queries, near_keys, near_values, tile_live, score_scale)

    attended, log_norm = lax.map(forward_one, (query_tiles, slot_ids, live_slots))
    attended_home = lax.all_to_all(
        attended.reshape(row_count, feat_count), "head", split_axis=0, concat_axis=1, tiled=True
    )
    row_delta = jnp.sum(
        cot_tiles.astype(jnp.float32) * attended.astype(jnp.float32), axis=-1
    ).transpose(0, 2, 1)
    grad_sum = jnp.zeros((2, row_count, feat_count), jnp.float32)

    def backward_one(inputs):
        tile_queries, tile_cot, tile_slots, tile_live, tile_norm, tile_delta = inputs
        near_keys = jnp.take(window[0], tile_slots, axis=0)
        near_values = jnp.take(window[1], tile_slots, axis=0)
        return tile_backward(
            tile_queries,
            tile_cot,
            near_keys,
            near_values,
            tile_live,
            tile_norm,
            tile_delta,
            score_scale,
        )

    query_grad, key_part, value_part = lax.map(
        backward_one, (query_tiles, cot_tiles, slot_ids, live_slots, log_norm, row_delta)
    )
    slot_flat = slot_ids.reshape(-1)
    live_flat = live_slots.reshape(-1)
    window_index = jnp.arange(window_tiles, dtype=jnp.int32)
    onehot = ((slot_flat[None, :] == window_index[:, None]) & live_flat[None, :]).astype(
        jnp.float32
    )
    both_parts = jnp.stack((key_part, value_part)).reshape(
        2, tiles_here * slot_count, TILE, feat_count
    )
    window_grad = jnp.einsum(
        "ws,csjf->cwjf",
        onehot,
        both_parts,
        precision=lax.Precision.HIGHEST,
        preferred_element_type=jnp.float32,
    ).astype(jnp.bfloat16)
    window_grad = lax.optimization_barrier(window_grad)
    for block_index in range(block_total):
        offset = dev_offsets[block_index]
        grad_piece = window_grad[
            :, block_index * tiles_here : (block_index + 1) * tiles_here
        ].reshape(2, row_count, feat_count)
        if offset != 0:
            grad_piece = shifted(grad_piece, "seq", offset)
        grad_sum = grad_sum + grad_piece.astype(jnp.float32)
    key_grad = grad_sum[0].astype(jnp.bfloat16)
    value_grad = grad_sum[1].astype(jnp.bfloat16)
    query_home, key_home, value_home = (
        lax.all_to_all(
            query_grad.reshape(row_count, feat_count),
            "head",
            split_axis=0,
            concat_axis=1,
            tiled=True,
        ),
        lax.all_to_all(key_grad, "head", split_axis=0, concat_axis=1, tiled=True),
        lax.all_to_all(value_grad, "head", split_axis=0, concat_axis=1, tiled=True),
    )
    return (attended_home, query_home, key_home, value_home)


def solution(mesh):
    placed = (
        P(("seq", "head"), None),
        P(("seq", "head"), None),
        P(("seq", "head"), None),
        P(("seq", "head"), None),
        P(),
    )
    return jax.shard_map(
        on_device,
        mesh=mesh,
        in_specs=placed,
        out_specs=(
            P(("seq", "head"), None),
            P(("seq", "head"), None),
            P(("seq", "head"), None),
            P(("seq", "head"), None),
        ),
        check_vma=False,
    )
```

profile of v0, /device:TPU:216, one launch (start us, length us, event | category | flops | bytes accessed | tf_op | source)
XLA Modules:
  0.0 386.3 jit_solution(10281116587870557805)
XLA Ops:
  2.4 7.6 %all-to-all-start.1 = ((bf16[96,4,384]{2,0,1:T(8,128)(2,1)}), bf16[96,4,384]{2,0,1:T(8,128)(2,1)S(1)}, u32[]{:S(2)}, u32[]{:S(2)}) async-start(bf16[96,4,384]{2,0,1:T(8,128)(2,1)} %bitcast.202), calls=%async_computation.1 | async-start | bytes 589824 | tf_op jit(solution)/shard_map/all_to_all | solution.py:119
  11.8 8.6 %all-to-all-done.1 = bf16[96,4,384]{2,0,1:T(8,128)(2,1)S(1)} async-done(((bf16[96,4,384]{2,0,1:T(8,128)(2,1)}), bf16[96,4,384]{2,0,1:T(8,128)(2,1)S(1)}, u32[]{:S(2)}, u32[]{:S(2)}) %all-to-all-start.1) | async-done | bytes 294944 | tf_op jit(solution)/shard_map/all_to_all | solution.py:119
  24.8 12.5 %all-to-all-done.2 = bf16[96,4,384]{2,0,1:T(8,128)(2,1)S(1)} async-done(((bf16[96,4,384]{2,0,1:T(8,128)(2,1)}), bf16[96,4,384]{2,0,1:T(8,128)(2,1)S(1)}, u32[]{:S(2)}, u32[]{:S(2)}) %all-to-all-start.2) | async-done | bytes 294944 | tf_op jit(solution)/shard_map/all_to_all | solution.py:120
  43.1 8.0 %all-to-all-done = bf16[96,4,384]{2,0,1:T(8,128)(2,1)S(1)} async-done(((bf16[96,4,384]{2,0,1:T(8,128)(2,1)}), bf16[96,4,384]{2,0,1:T(8,128)(2,1)S(1)}, u32[]{:S(2)}, u32[]{:S(2)}) %all-to-all-start) | async-done | bytes 294944 | tf_op jit(solution)/shard_map/all_to_all | solution.py:118
  57.2 8.9 %collective-permute-start.6 = (bf16[2,384,384]{2,1,0:T(8,128)(2,1)S(1)}, bf16[2,384,384]{2,1,0:T(8,128)(2,1)S(1)}, u32[]{:S(2)}, u32[]{:S(2)}) collective-permute-start(bf16[2,384,384]{2,1,0:T(8,128)(2,1)S(1)} %pad_maximum_fusion), channel_id=1, source_target_pairs={{256,0},{260,4},{264,8},{268,12},{272,16},{276,20},{280,24},{284,2... | collective-permute-start | bytes 1769480 | tf_op jit(solution)/shard_map/ppermute | solution.py:15
  69.5 9.2 %collective-permute-done = bf16[2,384,384]{2,1,0:T(8,128)(2,1)} collective-permute-done((bf16[2,384,384]{2,1,0:T(8,128)(2,1)S(1)}, bf16[2,384,384]{2,1,0:T(8,128)(2,1)}, u32[]{:S(2)}, u32[]{:S(2)}) %collective-permute-start) | collective-permute-done | bytes 589856 | tf_op jit(solution)/shard_map/ppermute | solution.py:15
  78.7 46.4 %collective-permute-start.3 = (bf16[2,384,384]{2,1,0:T(8,128)(2,1)S(1)}, bf16[2,384,384]{2,1,0:T(8,128)(2,1)S(1)}, u32[]{:S(2)}, u32[]{:S(2)}) collective-permute-start(bf16[2,384,384]{2,1,0:T(8,128)(2,1)S(1)} %pad_maximum_fusion), channel_id=1, source_target_pairs={{0,4},{4,8},{8,12},{12,16},{16,20},{20,24},{24,28},{28,32},{32,36}... | collective-permute-start | bytes 1769480 | tf_op jit(solution)/shard_map/ppermute | solution.py:15
  126.3 8.1 %collective-permute-done.1 = bf16[2,384,384]{2,1,0:T(8,128)(2,1)} collective-permute-done((bf16[2,384,384]{2,1,0:T(8,128)(2,1)S(1)}, bf16[2,384,384]{2,1,0:T(8,128)(2,1)}, u32[]{:S(2)}, u32[]{:S(2)}) %collective-permute-start.1) | collective-permute-done | bytes 589856 | tf_op jit(solution)/shard_map/ppermute | solution.py:15
  140.2 11.4 %collective-permute-done.4 = bf16[2,384,384]{2,1,0:T(8,128)(2,1)S(1)} collective-permute-done((bf16[2,384,384]{2,1,0:T(8,128)(2,1)S(1)}, bf16[2,384,384]{2,1,0:T(8,128)(2,1)S(1)}, u32[]{:S(2)}, u32[]{:S(2)}) %collective-permute-start.4) | collective-permute-done | bytes 589856 | tf_op jit(solution)/shard_map/ppermute | solution.py:15
  152.9 9.1 %collective-permute-done.7 = bf16[2,384,384]{2,1,0:T(8,128)(2,1)S(1)} collective-permute-done((bf16[2,384,384]{2,1,0:T(8,128)(2,1)S(1)}, bf16[2,384,384]{2,1,0:T(8,128)(2,1)S(1)}, u32[]{:S(2)}, u32[]{:S(2)}) %collective-permute-start.7) | collective-permute-done | bytes 589856 | tf_op jit(solution)/shard_map/ppermute | solution.py:15
  165.0 5.1 %copy.203 = bf16[1,9,384,384]{2,3,1,0:T(8,128)(2,1)S(1)} copy(bf16[1,9,384,384]{3,2,0,1:T(8,128)(2,1)} %get-tuple-element.320) | data formatting | bytes 5308416 | tf_op jit(solution)/shard_map/while/body/eval_jaxpr/slice | solution.py:160
  174.4 5.1 %copy.201 = bf16[1,9,384,384]{2,3,1,0:T(8,128)(2,1)S(1)} copy(bf16[1,9,384,384]{3,2,0,1:T(8,128)(2,1)} %get-tuple-element.321) | data formatting | bytes 5308416 | tf_op jit(solution)/shard_map/while/body/eval_jaxpr/slice | solution.py:159
  194.0 11.6 %while.47 = (s32[]{:T(128)}, bf16[3,384,128]{2,1,0:T(8,128)(2,1)S(1)}, f32[3,3,384,128]{2,3,0,1:T(8,128)}, f32[3,3,384,128]{2,3,0,1:T(8,128)}, pred[3]{0:T(512)(...) while((s32[]{:T(128)}, ...), condition=%wide.region_7.9_spmd, body=%wide.region_6.8_spmd.sunk | while | flops 569819136 | bytes 10534529 | solution.py:94
  212.5 9.5 %convert_bitcast_fusion = bf16[2,9,384,384]{3,1,2,0:T(8,128)(2,1)S(1)} fusion(f32[1,3,384,384]{3,1,2,0:T(4,128)S(1)} %copy.221, f32[1,3,384,384]{3,1,2,0:T(4,128)} %copy.220, s32[3]{0:T(128)S(1)} %get-tuple-element.306, pred[3]{0:T(512)(128)(4,1)S(1)} %get-tuple-element.536), kind=kOutput, calls=%fused_computation.53 | convolution fusion | flops 99090488 | bytes 8847375 | tf_op jit(solution)/shard_map/ws,csjf->cwjf/dot_general | solution.py:199
  222.0 8.5 %fusion.59 = (bf16[2,1,384,384]{3,1,2,0:T(2,128)(2,1)S(1)}, bf16[2,1,384,384]{3,1,2,0:T(2,128)(2,1)S(1)}, bf16[2,1,384,384]{3,1,2,0:T(2,128)(2,1)S(1)}, bf16[2,1...) fusion(bf16[2,9,384,384]{3,1,2,0:T(8,128)(2,1)S(1)} %convert_bi, ...), kind=kLoop, calls=%fused_computation.109 | loop fusion | flops 294912 | bytes 11206656 | tf_op jit(solution)/shard_map/slice | solution.py:209
  248.9 8.7 %collective-permute-start.9 = (bf16[2,384,384]{2,1,0:T(8,128)(2,1)}, bf16[2,384,384]{2,1,0:T(8,128)(2,1)}, u32[]{:S(2)}, u32[]{:S(2)}) collective-permute-start(bf16[2,384,384]{2,1,0:T(8,128)(2,1)} %bitcast.193), channel_id=1, source_target_pairs={{256,0},{260,4},{264,8},{268,12},{272,16},{276,20},{280,24},{284,2... | collective-permute-start | bytes 1769480 | tf_op jit(solution)/shard_map/ppermute | solution.py:15
  257.6 10.6 %collective-permute-done.15 = bf16[2,384,384]{2,1,0:T(8,128)(2,1)S(1)} collective-permute-done((bf16[2,384,384]{2,1,0:T(8,128)(2,1)S(1)}, bf16[2,384,384]{2,1,0:T(8,128)(2,1)S(1)}, u32[]{:S(2)}, u32[]{:S(2)}) %collective-permute-start.15) | collective-permute-done | bytes 589856 | tf_op jit(solution)/shard_map/ppermute | solution.py:15
  268.2 6.8 %collective-permute-start.10 = (bf16[2,384,384]{2,1,0:T(8,128)(2,1)}, bf16[2,384,384]{2,1,0:T(8,128)(2,1)}, u32[]{:S(2)}, u32[]{:S(2)}) collective-permute-start(bf16[2,384,384]{2,1,0:T(8,128)(2,1)} %bitcast.192), channel_id=1, source_target_pairs={{252,0},{256,4},{260,8},{264,12},{268,16},{272,20},{276,24},{280,2... | collective-permute-start | bytes 1769480 | tf_op jit(solution)/shard_map/ppermute | solution.py:15
  275.0 29.1 %collective-permute-done.14 = bf16[2,384,384]{2,1,0:T(8,128)(2,1)S(1)} collective-permute-done((bf16[2,384,384]{2,1,0:T(8,128)(2,1)S(1)}, bf16[2,384,384]{2,1,0:T(8,128)(2,1)S(1)}, u32[]{:S(2)}, u32[]{:S(2)}) %collective-permute-start.14) | collective-permute-done | bytes 589856 | tf_op jit(solution)/shard_map/ppermute | solution.py:15
  307.5 10.2 %all-to-all-start.5 = ((bf16[4,96,384]{2,1,0:T(8,128)(2,1)}), bf16[4,96,384]{2,1,0:T(8,128)(2,1)S(1)}, u32[]{:S(2)}, u32[]{:S(2)}) async-start(bf16[4,96,384]{2,1,0:T(8,128)(2,1)} %all_to_all.116), calls=%async_computation.5 | async-start | bytes 589824 | tf_op jit(solution)/shard_map/all_to_all | solution.py:218
  318.9 22.1 %all-to-all-done.5 = bf16[4,96,384]{2,1,0:T(8,128)(2,1)S(1)} async-done(((bf16[4,96,384]{2,1,0:T(8,128)(2,1)}), bf16[4,96,384]{2,1,0:T(8,128)(2,1)S(1)}, u32[]{:S(2)}, u32[]{:S(2)}) %all-to-all-start.5) | async-done | bytes 294944 | tf_op jit(solution)/shard_map/all_to_all | solution.py:218
  348.0 7.8 %all-to-all-done.3 = bf16[4,96,384]{2,1,0:T(8,128)(2,1)S(1)} async-done(((bf16[4,96,384]{2,1,0:T(8,128)(2,1)}), bf16[4,96,384]{2,1,0:T(8,128)(2,1)S(1)}, u32[]{:S(2)}, u32[]{:S(2)}) %all-to-all-start.3) | async-done | bytes 294944 | tf_op jit(solution)/shard_map/all_to_all | solution.py:164
  355.9 16.0 %all_to_all.134 = bf16[4,96,384]{2,1,0:T(8,128)(2,1)S(1)} all-to-all(bf16[4,96,384]{2,1,0:T(8,128)(2,1)S(1)} %bitcast.258), channel_id=1, replica_groups=mesh['seq'=128,'head'=4] {'head'}, dimensions={0} | all-to-all | bytes 589824 | tf_op jit(solution)/shard_map/all_to_all | solution.py:225
  377.5 8.0 %all-to-all-done.7 = bf16[4,96,384]{2,1,0:T(8,128)(2,1)S(1)} async-done(((bf16[4,96,384]{2,1,0:T(8,128)(2,1)}), bf16[4,96,384]{2,1,0:T(8,128)(2,1)S(1)}, u32[]{:S(2)}, u32[]{:S(2)}) %all-to-all-start.7) | async-done | bytes 294944 | tf_op jit(solution)/shard_map/all_to_all | solution.py:226
  (160 shorter events, 111.5 us)
Async XLA Ops:
  2.4 18.0 %all-to-all-start.1 = ((bf16[96,4,384]{2,0,1:T(8,128)(2,1)}), bf16[96,4,384]{2,0,1:T(8,128)(2,1)S(1)}, u32[]{:S(2)}, u32[]{:S(2)}) async-start(bf16[96,4,384]{2,0,1:T(8,128)(2,1)} %bitcast.202), calls=%async_computation.1 | async-start | bytes 589824 | tf_op jit(solution)/shard_map/all_to_all | solution.py:119
  20.4 16.9 %all-to-all-start.2 = ((bf16[96,4,384]{2,0,1:T(8,128)(2,1)}), bf16[96,4,384]{2,0,1:T(8,128)(2,1)S(1)}, u32[]{:S(2)}, u32[]{:S(2)}) async-start(bf16[96,4,384]{2,0,1:T(8,128)(2,1)} %bitcast.201), calls=%async_computation.2 | async-start | bytes 589824 | tf_op jit(solution)/shard_map/all_to_all | solution.py:120
  37.3 13.8 %all-to-all-start = ((bf16[96,4,384]{2,0,1:T(8,128)(2,1)}), bf16[96,4,384]{2,0,1:T(8,128)(2,1)S(1)}, u32[]{:S(2)}, u32[]{:S(2)}) async-start(bf16[96,4,384]{2,0,1:T(8,128)(2,1)} %bitcast.203), calls=%async_computation | async-start | bytes 589824 | tf_op jit(solution)/shard_map/all_to_all | solution.py:118
  41.1 37.7 %collective-permute-start = (bf16[2,384,384]{2,1,0:T(8,128)(2,1)S(1)}, bf16[2,384,384]{2,1,0:T(8,128)(2,1)}, u32[]{:S(2)}, u32[]{:S(2)}) collective-permute-start(bf16[2,384,384]{2,1,0:T(8,128)(2,1)S(1)} %pad_maximum_fusion), channel_id=1, source_target_pairs={{0,260},{4,264},{8,268},{12,272},{16,276},{20,280},{24,284},{28,28... | collective-permute-start | bytes 1769480 | tf_op jit(solution)/shard_map/ppermute | solution.py:15
  51.1 18.2 %all-to-all-start.4 = ((bf16[96,4,384]{2,0,1:T(8,128)(2,1)}), bf16[96,4,384]{2,0,1:T(8,128)(2,1)S(1)}, u32[]{:S(2)}, u32[]{:S(2)}) async-start(bf16[96,4,384]{2,0,1:T(8,128)(2,1)} %bitcast.200), calls=%async_computation.4 | async-start | bytes 589824 | tf_op jit(solution)/shard_map/all_to_all | solution.py:121
  54.6 79.7 %collective-permute-start.1 = (bf16[2,384,384]{2,1,0:T(8,128)(2,1)S(1)}, bf16[2,384,384]{2,1,0:T(8,128)(2,1)}, u32[]{:S(2)}, u32[]{:S(2)}) collective-permute-start(bf16[2,384,384]{2,1,0:T(8,128)(2,1)S(1)} %pad_maximum_fusion), channel_id=1, source_target_pairs={{0,256},{4,260},{8,264},{12,268},{16,272},{20,276},{24,280},{28,28... | collective-permute-start | bytes 1769480 | tf_op jit(solution)/shard_map/ppermute | solution.py:15
  55.9 81.5 %collective-permute-start.2 = (bf16[2,384,384]{2,1,0:T(8,128)(2,1)S(1)}, bf16[2,384,384]{2,1,0:T(8,128)(2,1)}, u32[]{:S(2)}, u32[]{:S(2)}) collective-permute-start(bf16[2,384,384]{2,1,0:T(8,128)(2,1)S(1)} %pad_maximum_fusion), channel_id=1, source_target_pairs={{0,252},{4,256},{8,260},{12,264},{16,268},{20,272},{24,276},{28,28... | collective-permute-start | bytes 1769480 | tf_op jit(solution)/shard_map/ppermute | solution.py:15
  57.2 95.6 %collective-permute-start.6 = (bf16[2,384,384]{2,1,0:T(8,128)(2,1)S(1)}, bf16[2,384,384]{2,1,0:T(8,128)(2,1)S(1)}, u32[]{:S(2)}, u32[]{:S(2)}) collective-permute-start(bf16[2,384,384]{2,1,0:T(8,128)(2,1)S(1)} %pad_maximum_fusion), channel_id=1, source_target_pairs={{256,0},{260,4},{264,8},{268,12},{272,16},{276,20},{280,24},{284,2... | collective-permute-start | bytes 1769480 | tf_op jit(solution)/shard_map/ppermute | solution.py:15
  66.2 85.5 %collective-permute-start.5 = (bf16[2,384,384]{2,1,0:T(8,128)(2,1)S(1)}, bf16[2,384,384]{2,1,0:T(8,128)(2,1)}, u32[]{:S(2)}, u32[]{:S(2)}) collective-permute-start(bf16[2,384,384]{2,1,0:T(8,128)(2,1)S(1)} %pad_maximum_fusion), channel_id=1, source_target_pairs={{252,0},{256,4},{260,8},{264,12},{268,16},{272,20},{276,24},{280,2... | collective-permute-start | bytes 1769480 | tf_op jit(solution)/shard_map/ppermute | solution.py:15
  78.7 61.2 %collective-permute-start.3 = (bf16[2,384,384]{2,1,0:T(8,128)(2,1)S(1)}, bf16[2,384,384]{2,1,0:T(8,128)(2,1)S(1)}, u32[]{:S(2)}, u32[]{:S(2)}) collective-permute-start(bf16[2,384,384]{2,1,0:T(8,128)(2,1)S(1)} %pad_maximum_fusion), channel_id=1, source_target_pairs={{0,4},{4,8},{8,12},{12,16},{16,20},{20,24},{24,28},{28,32},{32,36}... | collective-permute-start | bytes 1769480 | tf_op jit(solution)/shard_map/ppermute | solution.py:15
  134.4 17.2 %collective-permute-start.4 = (bf16[2,384,384]{2,1,0:T(8,128)(2,1)S(1)}, bf16[2,384,384]{2,1,0:T(8,128)(2,1)S(1)}, u32[]{:S(2)}, u32[]{:S(2)}) collective-permute-start(bf16[2,384,384]{2,1,0:T(8,128)(2,1)S(1)} %pad_maximum_fusion), channel_id=1, source_target_pairs={{4,0},{8,4},{12,8},{16,12},{20,16},{24,20},{28,24},{32,28},{36,32}... | collective-permute-start | bytes 1769480 | tf_op jit(solution)/shard_map/ppermute | solution.py:15
  137.4 24.5 %collective-permute-start.7 = (bf16[2,384,384]{2,1,0:T(8,128)(2,1)S(1)}, bf16[2,384,384]{2,1,0:T(8,128)(2,1)S(1)}, u32[]{:S(2)}, u32[]{:S(2)}) collective-permute-start(bf16[2,384,384]{2,1,0:T(8,128)(2,1)S(1)} %pad_maximum_fusion), channel_id=1, source_target_pairs={{260,0},{264,4},{268,8},{272,12},{276,16},{280,20},{284,24},{288,2... | collective-permute-start | bytes 1769480 | tf_op jit(solution)/shard_map/ppermute | solution.py:15
  232.3 16.7 %collective-permute-start.11 = (bf16[2,384,384]{2,1,0:T(8,128)(2,1)S(1)}, bf16[2,384,384]{2,1,0:T(8,128)(2,1)S(1)}, u32[]{:S(2)}, u32[]{:S(2)}) collective-permute-start(bf16[2,384,384]{2,1,0:T(8,128)(2,1)S(1)} %bitcast.262), channel_id=1, source_target_pairs={{4,0},{8,4},{12,8},{16,12},{20,16},{24,20},{28,24},{32,28},{36,32}... | collective-permute-start | bytes 1769480 | tf_op jit(solution)/shard_map/ppermute | solution.py:15
  234.2 34.0 %collective-permute-start.15 = (bf16[2,384,384]{2,1,0:T(8,128)(2,1)S(1)}, bf16[2,384,384]{2,1,0:T(8,128)(2,1)S(1)}, u32[]{:S(2)}, u32[]{:S(2)}) collective-permute-start(bf16[2,384,384]{2,1,0:T(8,128)(2,1)S(1)} %bitcast.260), channel_id=1, source_target_pairs={{0,260},{4,264},{8,268},{12,272},{16,276},{20,280},{24,284},{28,28... | collective-permute-start | bytes 1769480 | tf_op jit(solution)/shard_map/ppermute | solution.py:15
  235.6 68.5 %collective-permute-start.14 = (bf16[2,384,384]{2,1,0:T(8,128)(2,1)S(1)}, bf16[2,384,384]{2,1,0:T(8,128)(2,1)S(1)}, u32[]{:S(2)}, u32[]{:S(2)}) collective-permute-start(bf16[2,384,384]{2,1,0:T(8,128)(2,1)S(1)} %bitcast.261), channel_id=1, source_target_pairs={{0,256},{4,260},{8,264},{12,268},{16,272},{20,276},{24,280},{28,28... | collective-permute-start | bytes 1769480 | tf_op jit(solution)/shard_map/ppermute | solution.py:15
  240.8 76.9 %copy-start.6 = (bf16[3,384,128]{2,1,0:T(8,128)(2,1)S(1)}, bf16[3,384,128]{2,1,0:T(8,128)(2,1)}, u32[]{:S(2)}) copy-start(bf16[3,384,128]{2,1,0:T(8,128)(2,1)} %copy-done.5) | copy-start | bytes 884740
  241.7 102.8 %collective-permute-start.13 = (bf16[2,384,384]{2,1,0:T(8,128)(2,1)}, bf16[2,384,384]{2,1,0:T(8,128)(2,1)}, u32[]{:S(2)}, u32[]{:S(2)}) collective-permute-start(bf16[2,384,384]{2,1,0:T(8,128)(2,1)} %bitcast.197), channel_id=1, source_target_pairs={{0,252},{4,256},{8,260},{12,264},{16,268},{20,272},{24,276},{28,28... | collective-permute-start | bytes 1769480 | tf_op jit(solution)/shard_map/ppermute | solution.py:15
  243.0 101.5 %collective-permute-start.12 = (bf16[2,384,384]{2,1,0:T(8,128)(2,1)}, bf16[2,384,384]{2,1,0:T(8,128)(2,1)}, u32[]{:S(2)}, u32[]{:S(2)}) collective-permute-start(bf16[2,384,384]{2,1,0:T(8,128)(2,1)} %bitcast.198), channel_id=1, source_target_pairs={{0,4},{4,8},{8,12},{12,16},{16,20},{20,24},{24,28},{28,32},{32,36}... | collective-permute-start | bytes 1769480 | tf_op jit(solution)/shard_map/ppermute | solution.py:15
  248.9 95.5 %collective-permute-start.9 = (bf16[2,384,384]{2,1,0:T(8,128)(2,1)}, bf16[2,384,384]{2,1,0:T(8,128)(2,1)}, u32[]{:S(2)}, u32[]{:S(2)}) collective-permute-start(bf16[2,384,384]{2,1,0:T(8,128)(2,1)} %bitcast.193), channel_id=1, source_target_pairs={{256,0},{260,4},{264,8},{268,12},{272,16},{276,20},{280,24},{284,2... | collective-permute-start | bytes 1769480 | tf_op jit(solution)/shard_map/ppermute | solution.py:15
  268.2 76.3 %collective-permute-start.10 = (bf16[2,384,384]{2,1,0:T(8,128)(2,1)}, bf16[2,384,384]{2,1,0:T(8,128)(2,1)}, u32[]{:S(2)}, u32[]{:S(2)}) collective-permute-start(bf16[2,384,384]{2,1,0:T(8,128)(2,1)} %bitcast.192), channel_id=1, source_target_pairs={{252,0},{256,4},{260,8},{264,12},{268,16},{272,20},{276,24},{280,2... | collective-permute-start | bytes 1769480 | tf_op jit(solution)/shard_map/ppermute | solution.py:15
  304.1 40.4 %collective-permute-start.8 = (bf16[2,384,384]{2,1,0:T(8,128)(2,1)}, bf16[2,384,384]{2,1,0:T(8,128)(2,1)}, u32[]{:S(2)}, u32[]{:S(2)}) collective-permute-start(bf16[2,384,384]{2,1,0:T(8,128)(2,1)} %bitcast.194), channel_id=1, source_target_pairs={{260,0},{264,4},{268,8},{272,12},{276,16},{280,20},{284,24},{288,2... | collective-permute-start | bytes 1769480 | tf_op jit(solution)/shard_map/ppermute | solution.py:15
  307.5 33.5 %all-to-all-start.5 = ((bf16[4,96,384]{2,1,0:T(8,128)(2,1)}), bf16[4,96,384]{2,1,0:T(8,128)(2,1)S(1)}, u32[]{:S(2)}, u32[]{:S(2)}) async-start(bf16[4,96,384]{2,1,0:T(8,128)(2,1)} %all_to_all.116), calls=%async_computation.5 | async-start | bytes 589824 | tf_op jit(solution)/shard_map/all_to_all | solution.py:218
  341.0 14.9 %all-to-all-start.3 = ((bf16[4,96,384]{2,1,0:T(8,128)(2,1)}), bf16[4,96,384]{2,1,0:T(8,128)(2,1)S(1)}, u32[]{:S(2)}, u32[]{:S(2)}) async-start(bf16[4,96,384]{2,1,0:T(8,128)(2,1)} %all_to_all.109), calls=%async_computation.3 | async-start | bytes 589824 | tf_op jit(solution)/shard_map/all_to_all | solution.py:164
  371.8 13.7 %all-to-all-start.7 = ((bf16[4,96,384]{2,1,0:T(8,128)(2,1)}), bf16[4,96,384]{2,1,0:T(8,128)(2,1)S(1)}, u32[]{:S(2)}, u32[]{:S(2)}) async-start(bf16[4,96,384]{2,1,0:T(8,128)(2,1)} %bitcast.61), calls=%async_computation.7 | async-start | bytes 589824 | tf_op jit(solution)/shard_map/all_to_all | solution.py:226
  (16 other events, 469.2 us)
where the time goes:
time: 388 us; the launch traced here: 386 us
  waiting for transfers between devices  147 us (38%)
  starting transfers between devices  128 us (33%)
  local copies, waits for them, and re-layouts  57.2 us (15%)
  matrix products  23.7 us (6%)
  blocking collectives  16 us (4%)
  other arithmetic  13.4 us (3%)
    ppermute x16, starting transfers between devices, shifted(): return lax.ppermute(array, axis, pairs)  93 us
    ppermute x16, waiting for transfers between devices, shifted(): return lax.ppermute(array, axis, pairs)  79.5 us
    all_to_all x1, waiting for transfers between devices, on_device(): lax.all_to_all(query_grad.reshape(row_count, feat_count), 'head', split_a...  22.1 us
    all_to_all x1, blocking collectives, on_device(): lax.all_to_all(key_grad, 'head', split_axis=0, concat_axis=1, tiled=True)  16 us
    all_to_all x1, waiting for transfers between devices, on_device(): lax.all_to_all(value_rows, 'head', split_axis=1, concat_axis=0, tiled=True)  12.5 us
    unnamed x50, local copies, waits for them, and re-layouts  11.5 us
    all_to_all x1, starting transfers between devices, on_device(): lax.all_to_all(query_grad.reshape(row_count, feat_count), 'head', split_a...  10.2 us
    dot_general x1, matrix products, on_device(): jnp.einsum('ws,csjf->cwjf', onehot, both_parts, precision=lax.Precision.H...  9.53 us
  transfers between devices with their start and end apart: 23, of which 13 were waited for; matrix products, arithmetic and copies ran while one was open for 5% of the time, Pallas kernels for 0%

commit v1 on v0

v1 whole, which is shorter than its diff:
```python
import functools
import math

import jax
import jax.numpy as jnp
from jax import lax
from jax.experimental import pallas as pl
from jax.experimental.pallas import tpu as pltpu
from jax.sharding import PartitionSpec as P

HD = 128
TILE = 384
GRID_W = 4
QUARTERS = 4
MESH = pl.DeviceIdType.MESH


def dot(left, right, left_dim, right_dim):
    return lax.dot_general(
        left, right, (((left_dim,), (right_dim,)), ((), ())), preferred_element_type=jnp.float32
    )


def drain(ref, sem):
    pltpu.make_async_copy(ref, ref, sem).wait()


def kernel(heads, neigh, *refs):
    srcs = refs[0:4]
    outs = refs[4:8]
    refs = refs[8:]
    kw, vw, qb, cb = (refs[i * heads : (i + 1) * heads] for i in range(4))
    refs = refs[4 * heads :]
    staged, own, sib_send, sib_recv, x_send, x_recv = (
        refs[i * heads : (i + 1) * heads] for i in range(6)
    )
    refs = refs[6 * heads :]
    (zin_recv, zin_send, zin_own, xin_recv, xin_send, sin_recv, sin_send) = refs[:7]
    (sp_recv, sp_send, xp_recv, xp_send, out_recv, out_send, out_own) = refs[7:]

    seq, head = lax.axis_index("seq"), lax.axis_index("head")
    half = lax.axis_size("seq") // 2
    a, b, core = seq // half, head // 2, head % 2
    place = seq % half
    x = place % GRID_W
    rows = srcs[0].shape[0]
    block = pl.multiple_of(head * rows, rows)
    home = a == core

    def chip(a_to, b_to, core_to):
        return (a_to * half + place, b_to * 2 + core_to)

    def side(step):
        return (seq - x + (x + step + GRID_W) % GRID_W, head)

    sibling = (seq, b * 2 + 1 - core)

    barrier = pltpu.get_barrier_semaphore()
    partners = [
        chip((a + i) % 2, (b + m) % 2, (core + n) % 2)
        for i in range(2)
        for m in range(2)
        for n in range(2)
        if i + m + n > 0
    ] + [side(-1), side(1)]
    for partner in partners:
        pl.semaphore_signal(barrier, inc=1, device_id=partner, device_id_type=MESH)
    pl.semaphore_wait(barrier, len(partners))

    def remote(src, dst, send, recv, device):
        pltpu.make_async_remote_copy(
            src_ref=src, dst_ref=dst, send_sem=send, recv_sem=recv, device_id=device, device_id_type=MESH
        ).start()

    def columns(a_of, b_of, j):
        quarter = b_of * 2 + a_of
        return pl.ds(pl.multiple_of((quarter * heads + j) * HD, HD), HD)

    def gather(j, arrays):
        for i, m in ((1, 0), (1, 1), (0, 1), (0, 0)):
            a_to, b_to = (a + i) % 2, (b + m) % 2
            for n in arrays:
                src = srcs[n].at[:, columns(a_to, b_to, j)]
                dst = (kw[j].at[1], vw[j].at[1], qb[j], cb[j])[n].at[pl.ds(block, rows)]
                if i + m > 0:
                    remote(src, dst, zin_send.at[j], zin_recv.at[j, n], chip(a_to, b_to, a))
                else:

                    @pl.when(home)
                    def _():
                        pltpu.make_async_copy(src, dst, zin_recv.at[j, n]).start()

                    @pl.when(jnp.logical_not(home))
                    def _():
                        remote(src, dst, zin_own.at[j], zin_recv.at[j, n], sibling)

    def spread(j):
        drain(kw[j].at[1], zin_recv.at[j, 0])
        drain(vw[j].at[1], zin_recv.at[j, 1])
        for window in (kw[j], vw[j]):
            remote(window.at[1], window.at[2], xin_send.at[j], xin_recv.at[j, 1], side(-1))
            remote(window.at[1], window.at[0], xin_send.at[j], xin_recv.at[j, 0], side(1))
        for window in (kw[j], vw[j]):
            remote(window.at[1], window.at[4], sin_send.at[j], sin_recv.at[j], sibling)

    def relay(j):
        drain(kw[j].at[0:2], xin_recv.at[j, 0])
        drain(kw[j].at[0:2], xin_recv.at[j, 1])
        for window in (kw[j], vw[j]):
            remote(window.at[0], window.at[3], sin_send.at[j], sin_recv.at[j], sibling)
            remote(window.at[2], window.at[5], sin_send.at[j], sin_recv.at[j], sibling)

    def release(j, which):
        for i, m in ((0, 1), (1, 1), (1, 0), (0, 0)):
            b_to, core_to = (b + i) % 2, (core + m) % 2
            for n in which:
                src = staged[j].at[n, pl.ds(pl.multiple_of((b_to * 2 + core_to) * rows, rows), rows)]
                dst = outs[n].at[:, columns(a, b, j)]
                if i + m > 0:
                    remote(src, dst, out_send.at[j], out_recv.at[n], chip(core, b_to, core_to))
                else:

                    @pl.when(home)
                    def _():
                        pltpu.make_async_copy(src, dst, out_recv.at[n]).start()

                    @pl.when(jnp.logical_not(home))
                    def _():
                        remote(src, dst, out_own.at[j], out_recv.at[n], chip(core, b_to, core_to))

    tile = core * half + place
    slots, gaps = [1], [jnp.float32(0.0)]
    for n in (1, 2):
        other = neigh[tile, n]
        live = other >= 0
        safe = jnp.where(live, other, tile)
        away = jnp.where(lax.div(safe, half) == core, 0, 3)
        slots.append(jnp.clip(away + lax.rem(safe, GRID_W) - x + 1, 0, 5))
        gaps.append(jnp.where(live, jnp.float32(0.0), jnp.float32(1e30)))
    scale = 1.0 / math.sqrt(HD)
    rate = scale * math.log2(math.e)

    def attend(j):
        drain(qb[j], zin_recv.at[j, 2])
        drain(cb[j], zin_recv.at[j, 3])
        drain(kw[j], sin_recv.at[j])
        queries, cot = qb[j][...], cb[j][...]
        keys = [kw[j][slot] for slot in slots]
        values = [vw[j][slot] for slot in slots]
        raw = [dot(key, queries, 1, 1) for key in keys]
        top = jnp.max(raw[0], axis=0, keepdims=True)
        for n in (1, 2):
            top = jnp.maximum(top, jnp.max(raw[n], axis=0, keepdims=True) - gaps[n])
        shifted = [top * rate + gap for gap in gaps]
        powers = [jnp.exp2(raw[n] * rate - shifted[n]) for n in range(3)]
        total = sum(jnp.sum(power, axis=0, keepdims=True) for power in powers)
        inverse = 1.0 / total
        probs = [power * inverse for power in powers]
        probs_low = [prob.astype(jnp.bfloat16) for prob in probs]
        attended = sum(dot(values[n], probs_low[n], 0, 0) for n in range(3))
        attended_low = attended.T.astype(jnp.bfloat16)
        staged[j][0] = attended_low
        delta = jnp.sum(
            cot.astype(jnp.float32) * attended_low.astype(jnp.float32), axis=1, keepdims=True
        )
        delta = delta.reshape(1, TILE)
        query_grad = jnp.zeros((HD, TILE), jnp.float32)
        key_parts, value_parts = [], []
        for n in range(3):
            prob_grad = dot(values[n], cot, 1, 1)
            dscore = (probs[n] * (prob_grad - delta) * scale).astype(jnp.bfloat16)
            query_grad += dot(keys[n], dscore, 0, 0)
            key_parts.append(dot(dscore, queries, 1, 0))
            value_parts.append(dot(probs_low[n], cot, 1, 0))
        staged[j][1] = query_grad.T.astype(jnp.bfloat16)
        release(j, (0, 1))
        for which, parts in enumerate((key_parts, value_parts)):
            own[j][which, 1] = parts[0]
            for slot in (0, 2, 3, 4, 5):
                part = jnp.where(slots[1] == slot, parts[1], 0.0) + jnp.where(
                    slots[2] == slot, parts[2], 0.0
                )
                if slot < 3:
                    own[j][which, slot] = part
                else:
                    sib_send[j][which, slot - 3] = part.astype(jnp.bfloat16)
        remote(sib_send[j], sib_recv[j], sp_send.at[j], sp_recv.at[j], sibling)

    def give(j):
        drain(sib_recv[j], sp_recv.at[j])
        for way, slot in ((0, 0), (1, 2)):
            for which in range(2):
                x_send[j][way, which] = (
                    own[j][which, slot] + sib_recv[j][which, slot].astype(jnp.float32)
                ).astype(jnp.bfloat16)
        remote(x_send[j].at[0], x_recv[j].at[0], xp_send.at[j], xp_recv.at[j, 0], side(-1))
        remote(x_send[j].at[1], x_recv[j].at[1], xp_send.at[j], xp_recv.at[j, 1], side(1))

    def finish(j):
        drain(x_recv[j].at[0], xp_recv.at[j, 0])
        drain(x_recv[j].at[1], xp_recv.at[j, 1])
        for which in range(2):
            total = own[j][which, 1] + sib_recv[j][which, 1].astype(jnp.float32)
            total += x_recv[j][0, which].astype(jnp.float32)
            total += x_recv[j][1, which].astype(jnp.float32)
            staged[j][2 + which] = total.astype(jnp.bfloat16)
        release(j, (2, 3))

    for j in range(heads):
        gather(j, (0, 1))
        gather(j, (2, 3))
    spread(0)
    relay(0)
    spread(1)
    attend(0)
    relay(1)
    give(0)
    spread(2)
    attend(1)
    finish(0)
    relay(2)
    give(1)
    attend(2)
    finish(1)
    give(2)
    finish(2)

    for j in range(heads):
        drain(kw[j].at[0:3], zin_send.at[j])
        drain(kw[j].at[0:4], xin_send.at[j])
        drain(kw[j], sin_send.at[j])
        drain(sib_send[j], sp_send.at[j])
        drain(x_send[j], xp_send.at[j])
        drain(kw[j].at[0:3], out_send.at[j])

        @pl.when(jnp.logical_not(home))
        def _():
            drain(kw[j].at[0], zin_own.at[j])
            drain(kw[j].at[0], out_own.at[j])

    for n in range(4):
        drain(outs[n], out_recv.at[n])


def on_device(query_rows, key_rows, value_rows, cotangent, neighbours):
    rows, feat = query_rows.shape
    heads = feat // HD // QUARTERS
    low, wide = jnp.bfloat16, jnp.float32
    dma = pltpu.SemaphoreType.DMA
    scratch = []
    for shape, dtype in (
        ((6, TILE, HD), low),
        ((6, TILE, HD), low),
        ((TILE, HD), low),
        ((TILE, HD), low),
        ((4, TILE, HD), low),
        ((2, 3, TILE, HD), wide),
        ((2, 3, TILE, HD), low),
        ((2, 3, TILE, HD), low),
        ((2, 2, TILE, HD), low),
        ((2, 2, TILE, HD), low),
    ):
        scratch += [pltpu.VMEM(shape, dtype)] * heads
    scratch += [dma((heads, 4)), dma((heads,)), dma((heads,)), dma((heads, 2)), dma((heads,))]
    scratch += [dma((heads,)), dma((heads,)), dma((heads,)), dma((heads,)), dma((heads, 2))]
    scratch += [dma((heads,)), dma((4,)), dma((heads,)), dma((heads,))]
    anywhere = pl.BlockSpec(memory_space=pl.ANY)
    work = heads * TILE * 3 * TILE
    return tuple(
        pl.pallas_call(
            functools.partial(kernel, heads),
            out_shape=[jax.ShapeDtypeStruct((rows, feat), low)] * 4,
            in_specs=[pl.BlockSpec(memory_space=pltpu.SMEM)] + [anywhere] * 4,
            out_specs=[anywhere] * 4,
            scratch_shapes=scratch,
            compiler_params=pltpu.CompilerParams(
                collective_id=0, has_side_effects=True, vmem_limit_bytes=48 << 20
            ),
            cost_estimate=pl.CostEstimate(
                flops=work * HD * 12, bytes_accessed=rows * feat * 16, transcendentals=work
            ),
            name="tile_attention",
        )(neighbours, key_rows, value_rows, query_rows, cotangent)
    )


def solution(mesh):
    placed = P(("seq", "head"), None)
    return jax.shard_map(
        on_device,
        mesh=mesh,
        in_specs=(placed, placed, placed, placed, P()),
        out_specs=(placed, placed, placed, placed),
        check_vma=False,
    )
```

time: 388 us -> 87.4 us (0.23)
  the two profiles are of different devices: /device:TPU:216 before, /device:TPU:112 now
where the time goes in v1:
time: 87.4 us; the launch traced here: 87.1 us
  Pallas kernels  79 us (90%)
  local copies, waits for them, and re-layouts  7.48 us (9%)
    pallas_call x1, Pallas kernels, on_device(): pl.pallas_call(functools.partial(kernel, heads), out_shape=[jax.ShapeDtyp...  79 us
    unnamed x13, local copies, waits for them, and re-layouts  7.48 us

profile of v1, /device:TPU:112, one launch (start us, length us, event | category | flops | bytes accessed | tf_op | source)
XLA Modules:
  0.0 87.1 jit_solution(15112327351691767233)
XLA Ops:
  0.6 0.8 copy.9.neigh
  1.4 0.0 copy-start
  1.4 1.0 %copy-done = bf16[96,1536]{1,0:T(8,128)(2,1)S(1)} copy-done((bf16[96,1536]{1,0:T(8,128)(2,1)S(1)}, bf16[96,1536]{1,0:T(8,128)(2,1)}, u32[]{:S(2)}) %copy-start) | copy-done | bytes 294936
  2.4 0.0 copy-start.1
  2.4 1.0 %copy-done.1 = bf16[96,1536]{1,0:T(8,128)(2,1)S(1)} copy-done((bf16[96,1536]{1,0:T(8,128)(2,1)S(1)}, bf16[96,1536]{1,0:T(8,128)(2,1)}, u32[]{:S(2)}) %copy-start.1) | copy-done | bytes 294936
  3.3 0.0 copy-start.2
  3.3 1.0 %copy-done.2 = bf16[96,1536]{1,0:T(8,128)(2,1)S(1)} copy-done((bf16[96,1536]{1,0:T(8,128)(2,1)S(1)}, bf16[96,1536]{1,0:T(8,128)(2,1)}, u32[]{:S(2)}) %copy-start.2) | copy-done | bytes 294936
  4.3 0.0 copy-start.3
  4.3 1.0 %copy-done.3 = bf16[96,1536]{1,0:T(8,128)(2,1)S(1)} copy-done((bf16[96,1536]{1,0:T(8,128)(2,1)S(1)}, bf16[96,1536]{1,0:T(8,128)(2,1)}, u32[]{:S(2)}) %copy-start.3) | copy-done | bytes 294936
  5.3 79.0 %tile_attention.1 = (bf16[96,1536]{1,0:T(8,128)(2,1)S(1)}, bf16[96,1536]{1,0:T(8,128)(2,1)S(1)}, bf16[96,1536]{1,0:T(8,128)(2,1)S(1)}, bf16[96,1536]{1,0:T(8,128)(2,1)S(1)}) custom-call(s32[128,3]{1,0:T(8,128)S(1)} %copy.9.neigh, bf16[96,1536]{1,0:T(8,128)(2,1)S(1)} %copy-done, bf16[96,1536]{1,0:T(8,128)(2,1)S(1)} %copy-done.1, ...), custom_call_target="tpu_custom_call" | custom-call | flops 2038431744 | bytes 2359296 | tf_op jit(solution)/shard_map/tile_attention/pallas_call | solution.py:270
  84.3 0.7 copy.14
  85.0 0.7 copy.15
  85.7 0.7 copy.16
  86.4 0.7 copy.17
Async XLA Ops:
  1.4 1.0 %copy-start = (bf16[96,1536]{1,0:T(8,128)(2,1)S(1)}, bf16[96,1536]{1,0:T(8,128)(2,1)}, u32[]{:S(2)}) copy-start(bf16[96,1536]{1,0:T(8,128)(2,1)} %refs_0_.1) | copy-start | bytes 884740
  2.4 1.0 %copy-start.1 = (bf16[96,1536]{1,0:T(8,128)(2,1)S(1)}, bf16[96,1536]{1,0:T(8,128)(2,1)}, u32[]{:S(2)}) copy-start(bf16[96,1536]{1,0:T(8,128)(2,1)} %refs_1_.1) | copy-start | bytes 884740
  3.3 1.0 %copy-start.2 = (bf16[96,1536]{1,0:T(8,128)(2,1)S(1)}, bf16[96,1536]{1,0:T(8,128)(2,1)}, u32[]{:S(2)}) copy-start(bf16[96,1536]{1,0:T(8,128)(2,1)} %refs_2_.1) | copy-start | bytes 884740
  4.3 1.0 %copy-start.3 = (bf16[96,1536]{1,0:T(8,128)(2,1)S(1)}, bf16[96,1536]{1,0:T(8,128)(2,1)}, u32[]{:S(2)}) copy-start(bf16[96,1536]{1,0:T(8,128)(2,1)} %refs_3_.1) | copy-start | bytes 884740

commit v2 on v1

--- a/solution.py
+++ b/solution.py
@@ -12,6 +12,7 @@
 TILE = 384
 GRID_W = 4
 QUARTERS = 4
+VMEM = 60 << 20
 MESH = pl.DeviceIdType.MESH
 
 
@@ -27,8 +28,8 @@
 
 def kernel(heads, neigh, *refs):
     srcs = refs[0:4]
-    outs = refs[4:8]
-    refs = refs[8:]
+    outs = [refs[4].at[n] for n in range(4)]
+    refs = refs[5:]
     kw, vw, qb, cb = (refs[i * heads : (i + 1) * heads] for i in range(4))
     refs = refs[4 * heads :]
     staged, own, sib_send, sib_recv, x_send, x_recv = (
@@ -94,9 +95,11 @@
                     def _():
                         remote(src, dst, zin_own.at[j], zin_recv.at[j, n], sibling)
 
+    def arrive(j, arrays):
+        for n in arrays:
+            drain(qb[j], zin_recv.at[j, n])
+
     def spread(j):
-        drain(kw[j].at[1], zin_recv.at[j, 0])
-        drain(vw[j].at[1], zin_recv.at[j, 1])
         for window in (kw[j], vw[j]):
             remote(window.at[1], window.at[2], xin_send.at[j], xin_recv.at[j, 1], side(-1))
             remote(window.at[1], window.at[0], xin_send.at[j], xin_recv.at[j, 0], side(1))
@@ -131,7 +134,7 @@
     tile = core * half + place
     slots, gaps = [1], [jnp.float32(0.0)]
     for n in (1, 2):
-        other = neigh[tile, n]
+        other = neigh[n, tile]
         live = other >= 0
         safe = jnp.where(live, other, tile)
         away = jnp.where(lax.div(safe, half) == core, 0, 3)
@@ -141,8 +144,6 @@
     rate = scale * math.log2(math.e)
 
     def attend(j):
-        drain(qb[j], zin_recv.at[j, 2])
-        drain(cb[j], zin_recv.at[j, 3])
         drain(kw[j], sin_recv.at[j])
         queries, cot = qb[j][...], cb[j][...]
         keys = [kw[j][slot] for slot in slots]
@@ -206,20 +207,30 @@
             staged[j][2 + which] = total.astype(jnp.bfloat16)
         release(j, (2, 3))
 
-    for j in range(heads):
-        gather(j, (0, 1))
-        gather(j, (2, 3))
+    sides, middles = (0, 1), (2, 3)
+    gather(0, sides)
+    gather(0, middles)
+    arrive(0, sides)
+    gather(1, sides)
     spread(0)
+    arrive(0, middles)
+    gather(2, sides)
     relay(0)
+    attend(0)
+    arrive(1, sides)
+    gather(1, middles)
     spread(1)
-    attend(0)
+    arrive(2, sides)
+    gather(2, middles)
+    spread(2)
+    give(0)
     relay(1)
-    give(0)
-    spread(2)
+    arrive(1, middles)
     attend(1)
     finish(0)
     relay(2)
     give(1)
+    arrive(2, middles)
     attend(2)
     finish(1)
     give(2)
@@ -265,23 +276,24 @@
     scratch += [dma((heads,)), dma((heads,)), dma((heads,)), dma((heads,)), dma((heads, 2))]
     scratch += [dma((heads,)), dma((4,)), dma((heads,)), dma((heads,))]
     anywhere = pl.BlockSpec(memory_space=pl.ANY)
+    hbm = pl.BlockSpec(memory_space=pltpu.HBM)
     work = heads * TILE * 3 * TILE
-    return tuple(
-        pl.pallas_call(
+    shapes = jax.ShapeDtypeStruct((4, rows, feat), low)
+    landed = pl.pallas_call(
             functools.partial(kernel, heads),
-            out_shape=[jax.ShapeDtypeStruct((rows, feat), low)] * 4,
-            in_specs=[pl.BlockSpec(memory_space=pltpu.SMEM)] + [anywhere] * 4,
-            out_specs=[anywhere] * 4,
+            out_shape=shapes,
+            in_specs=[pl.BlockSpec(memory_space=pltpu.SMEM)] + [hbm] * 4,
+            out_specs=anywhere,
             scratch_shapes=scratch,
             compiler_params=pltpu.CompilerParams(
-                collective_id=0, has_side_effects=True, vmem_limit_bytes=48 << 20
+                collective_id=0, has_side_effects=True, vmem_limit_bytes=VMEM
             ),
             cost_estimate=pl.CostEstimate(
                 flops=work * HD * 12, bytes_accessed=rows * feat * 16, transcendentals=work
             ),
             name="tile_attention",
-        )(neighbours, key_rows, value_rows, query_rows, cotangent)
-    )
+        )(neighbours.T, key_rows, value_rows, query_rows, cotangent)
+    return landed[0], landed[1], landed[2], landed[3]
 
 
 def solution(mesh):

time: 87.4 us -> 71.5 us (0.82)
  the two profiles are of different devices: /device:TPU:112 before, /device:TPU:56 now
where the time goes in v2:
time: 71.5 us; the launch traced here: 71.3 us
  Pallas kernels  68.4 us (96%)
  local copies, waits for them, and re-layouts  2.26 us (3%)
    pallas_call x1, Pallas kernels, on_device(): pl.pallas_call(functools.partial(kernel, heads), out_shape=shapes, in_spe...  68.4 us
    squeeze x1, local copies, waits for them, and re-layouts, on_device(): return (landed[0], landed[1], landed[2], landed[3])  2.26 us

profile of v2, /device:TPU:56, one launch (start us, length us, event | category | flops | bytes accessed | tf_op | source)
XLA Modules:
  0.0 71.3 jit_solution(5551922259985865476)
XLA Ops:
  0.6 68.4 %tile_attention.1 = bf16[4,96,1536]{2,1,0:T(8,128)(2,1)} custom-call(s32[3,128]{1,0:T(4,128)} %bitcast.9, bf16[96,1536]{1,0:T(8,128)(2,1)} %refs_0_.1, bf16[96,1536]{1,0:T(8,128)(2,1)} %refs_1_.1, bf16[96,1536]{1,0:T(8,128)(2,1)} %refs_2_.1, bf16[96,1536]{1,0:T(8,128)(2,1)} %refs_3_.1), custom_call_target="tpu_custom_call" | custom-call | flops 2038431744 | bytes 2359296 | tf_op jit(solution)/shard_map/tile_attention/pallas_call | solution.py:282
  69.0 2.3 %slice_bitcast_fusion = (bf16[96,1536]{1,0:T(8,128)(2,1)}, bf16[96,1536]{1,0:T(8,128)(2,1)}, bf16[96,1536]{1,0:T(8,128)(2,1)}, bf16[96,1536]{1,0:T(8,128)(2,1)}) fusion(bf16[4,96,1536]{2,1,0:T(8,128)(2,1)} %tile_attention.1), kind=kLoop, calls=%fused_computation | loop fusion | bytes 2359296 | tf_op jit(solution)/shard_map/squeeze | solution.py:296

commit v3 on v2

--- a/solution.py
+++ b/solution.py
@@ -12,7 +12,7 @@
 TILE = 384
 GRID_W = 4
 QUARTERS = 4
-VMEM = 60 << 20
+VMEM = 58 << 20
 MESH = pl.DeviceIdType.MESH
 
 
@@ -26,7 +26,7 @@
     pltpu.make_async_copy(ref, ref, sem).wait()
 
 
-def kernel(heads, neigh, *refs):
+def kernel(heads, neigh_hbm, *refs):
     srcs = refs[0:4]
     outs = [refs[4].at[n] for n in range(4)]
     refs = refs[5:]
@@ -37,7 +37,8 @@
     )
     refs = refs[6 * heads :]
     (zin_recv, zin_send, zin_own, xin_recv, xin_send, sin_recv, sin_send) = refs[:7]
-    (sp_recv, sp_send, xp_recv, xp_send, out_recv, out_send, out_own) = refs[7:]
+    (sp_recv, sp_send, xp_recv, xp_send, out_recv, out_send, out_own) = refs[7:14]
+    neigh, neigh_sem = refs[14:]
 
     seq, head = lax.axis_index("seq"), lax.axis_index("head")
     half = lax.axis_size("seq") // 2
@@ -66,6 +67,8 @@
     ] + [side(-1), side(1)]
     for partner in partners:
         pl.semaphore_signal(barrier, inc=1, device_id=partner, device_id_type=MESH)
+    neigh_copy = pltpu.make_async_copy(neigh_hbm, neigh, neigh_sem)
+    neigh_copy.start()
     pl.semaphore_wait(barrier, len(partners))
 
     def remote(src, dst, send, recv, device):
@@ -78,7 +81,7 @@
         return pl.ds(pl.multiple_of((quarter * heads + j) * HD, HD), HD)
 
     def gather(j, arrays):
-        for i, m in ((1, 0), (1, 1), (0, 1), (0, 0)):
+        for i, m in ((0, 1), (1, 0), (1, 1), (0, 0)):
             a_to, b_to = (a + i) % 2, (b + m) % 2
             for n in arrays:
                 src = srcs[n].at[:, columns(a_to, b_to, j)]
@@ -114,7 +117,7 @@
             remote(window.at[2], window.at[5], sin_send.at[j], sin_recv.at[j], sibling)
 
     def release(j, which):
-        for i, m in ((0, 1), (1, 1), (1, 0), (0, 0)):
+        for i, m in ((1, 1), (1, 0), (0, 1), (0, 0)):
             b_to, core_to = (b + i) % 2, (core + m) % 2
             for n in which:
                 src = staged[j].at[n, pl.ds(pl.multiple_of((b_to * 2 + core_to) * rows, rows), rows)]
@@ -131,6 +134,10 @@
                     def _():
                         remote(src, dst, out_own.at[j], out_recv.at[n], chip(core, b_to, core_to))
 
+    scale = 1.0 / math.sqrt(HD)
+    rate = scale * math.log2(math.e)
+
+    neigh_copy.wait()
     tile = core * half + place
     slots, gaps = [1], [jnp.float32(0.0)]
     for n in (1, 2):
@@ -140,8 +147,6 @@
         away = jnp.where(lax.div(safe, half) == core, 0, 3)
         slots.append(jnp.clip(away + lax.rem(safe, GRID_W) - x + 1, 0, 5))
         gaps.append(jnp.where(live, jnp.float32(0.0), jnp.float32(1e30)))
-    scale = 1.0 / math.sqrt(HD)
-    rate = scale * math.log2(math.e)
 
     def attend(j):
         drain(kw[j], sin_recv.at[j])
@@ -174,7 +179,6 @@
             key_parts.append(dot(dscore, queries, 1, 0))
             value_parts.append(dot(probs_low[n], cot, 1, 0))
         staged[j][1] = query_grad.T.astype(jnp.bfloat16)
-        release(j, (0, 1))
         for which, parts in enumerate((key_parts, value_parts)):
             own[j][which, 1] = parts[0]
             for slot in (0, 2, 3, 4, 5):
@@ -205,7 +209,6 @@
             total += x_recv[j][0, which].astype(jnp.float32)
             total += x_recv[j][1, which].astype(jnp.float32)
             staged[j][2 + which] = total.astype(jnp.bfloat16)
-        release(j, (2, 3))
 
     sides, middles = (0, 1), (2, 3)
     gather(0, sides)
@@ -216,25 +219,31 @@
     arrive(0, middles)
     gather(2, sides)
     relay(0)
-    attend(0)
     arrive(1, sides)
     gather(1, middles)
     spread(1)
+    attend(0)
     arrive(2, sides)
     gather(2, middles)
     spread(2)
+    release(0, sides)
     give(0)
     relay(1)
     arrive(1, middles)
     attend(1)
+    release(1, sides)
+    relay(2)
     finish(0)
-    relay(2)
+    release(0, middles)
     give(1)
     arrive(2, middles)
     attend(2)
+    release(2, sides)
+    give(2)
     finish(1)
-    give(2)
+    release(1, middles)
     finish(2)
+    release(2, middles)
 
     for j in range(heads):
         drain(kw[j].at[0:3], zin_send.at[j])
@@ -275,14 +284,16 @@
     scratch += [dma((heads, 4)), dma((heads,)), dma((heads,)), dma((heads, 2)), dma((heads,))]
     scratch += [dma((heads,)), dma((heads,)), dma((heads,)), dma((heads,)), dma((heads, 2))]
     scratch += [dma((heads,)), dma((4,)), dma((heads,)), dma((heads,))]
+    scratch += [pltpu.SMEM(neighbours.shape[::-1], jnp.int32), dma]
     anywhere = pl.BlockSpec(memory_space=pl.ANY)
     hbm = pl.BlockSpec(memory_space=pltpu.HBM)
     work = heads * TILE * 3 * TILE
-    shapes = jax.ShapeDtypeStruct((4, rows, feat), low)
+    shapes = pltpu.VMEM((4, rows, feat), low)
+    sources = (neighbours.T, key_rows, value_rows, query_rows, cotangent)
     landed = pl.pallas_call(
             functools.partial(kernel, heads),
             out_shape=shapes,
-            in_specs=[pl.BlockSpec(memory_space=pltpu.SMEM)] + [hbm] * 4,
+            in_specs=[hbm] * 5,
             out_specs=anywhere,
             scratch_shapes=scratch,
             compiler_params=pltpu.CompilerParams(
@@ -292,7 +303,7 @@
                 flops=work * HD * 12, bytes_accessed=rows * feat * 16, transcendentals=work
             ),
             name="tile_attention",
-        )(neighbours.T, key_rows, value_rows, query_rows, cotangent)
+        )(*(pltpu.with_memory_space_constraint(source, pltpu.HBM) for source in sources))
     return landed[0], landed[1], landed[2], landed[3]
 
 

time: 71.5 us -> 67.4 us (0.943)
  Pallas kernels: 68.4 us -> 65.6 us
  local copies, waits for them, and re-layouts: 2.26 us -> 1.03 us
    pallas_call x1, Pallas kernels: 68.4 us -> 65.6 us  [on_device(): pl.pallas_call(functools.partial(kernel, heads), out_shape=shapes, in_spe...]
    squeeze x1, local copies, waits for them, and re-layouts: 2.26 us -> 1.03 us  [on_device(): return (landed[0], landed[1], landed[2], landed[3])]
where the time goes in v3:
time: 67.4 us; the launch traced here: 67.2 us
  Pallas kernels  65.6 us (97%)
  local copies, waits for them, and re-layouts  1.03 us (2%)
    pallas_call x1, Pallas kernels, on_device(): pl.pallas_call(functools.partial(kernel, heads), out_shape=shapes, in_spe...  65.6 us

profile of v3, /device:TPU:56, one launch (start us, length us, event | category | flops | bytes accessed | tf_op | source)
XLA Modules:
  0.0 67.2 jit_solution(5226848918483387329)
XLA Ops:
  0.6 65.6 %tile_attention.1 = bf16[4,96,1536]{2,1,0:T(8,128)(2,1)S(1)} custom-call(s32[3,128]{1,0:T(4,128)} %bitcast.9, bf16[96,1536]{1,0:T(8,128)(2,1)} %refs_0_.1, bf16[96,1536]{1,0:T(8,128)(2,1)} %refs_1_.1, bf16[96,1536]{1,0:T(8,128)(2,1)} %refs_2_.1, bf16[96,1536]{1,0:T(8,128)(2,1)} %refs_3_.1), custom_call_target="tpu_custom_call" | custom-call | flops 2038431744 | bytes 2359296 | tf_op jit(solution)/shard_map/tile_attention/pallas_call | solution.py:293
  66.2 1.0 %slice_bitcast_fusion = (bf16[96,1536]{1,0:T(8,128)(2,1)}, bf16[96,1536]{1,0:T(8,128)(2,1)}, bf16[96,1536]{1,0:T(8,128)(2,1)}, bf16[96,1536]{1,0:T(8,128)(2,1)}) fusion(bf16[4,96,1536]{2,1,0:T(8,128)(2,1)S(1)} %tile_attention.1), kind=kLoop, calls=%fused_computation | loop fusion | bytes 2359296 | tf_op jit(solution)/shard_map/squeeze | solution.py:307

commit v4 on v3

--- a/solution.py
+++ b/solution.py
@@ -37,8 +37,8 @@
     )
     refs = refs[6 * heads :]
     (zin_recv, zin_send, zin_own, xin_recv, xin_send, sin_recv, sin_send) = refs[:7]
-    (sp_recv, sp_send, xp_recv, xp_send, out_recv, out_send, out_own) = refs[7:14]
-    neigh, neigh_sem = refs[14:]
+    (sp_recv, sp_send, xp_recv, xp_send, out_recv, out_send) = refs[7:13]
+    neigh, neigh_sem = refs[13:]
 
     seq, head = lax.axis_index("seq"), lax.axis_index("head")
     half = lax.axis_size("seq") // 2
@@ -117,36 +117,39 @@
             remote(window.at[2], window.at[5], sin_send.at[j], sin_recv.at[j], sibling)
 
     def release(j, which):
-        for i, m in ((1, 1), (1, 0), (0, 1), (0, 0)):
-            b_to, core_to = (b + i) % 2, (core + m) % 2
+        for b_to, m in ((0, 1), (0, 0), (1, 1), (1, 0)):
+            core_to = (core + m) % 2
             for n in which:
                 src = staged[j].at[n, pl.ds(pl.multiple_of((b_to * 2 + core_to) * rows, rows), rows)]
                 dst = outs[n].at[:, columns(a, b, j)]
-                if i + m > 0:
+                if m > 0:
                     remote(src, dst, out_send.at[j], out_recv.at[n], chip(core, b_to, core_to))
                 else:
-
-                    @pl.when(home)
+                    stays = jnp.logical_and(home, b == b_to)
+
+                    @pl.when(stays)
                     def _():
                         pltpu.make_async_copy(src, dst, out_recv.at[n]).start()
 
-                    @pl.when(jnp.logical_not(home))
+                    @pl.when(jnp.logical_not(stays))
                     def _():
-                        remote(src, dst, out_own.at[j], out_recv.at[n], chip(core, b_to, core_to))
+                        remote(src, dst, out_send.at[j], out_recv.at[n], chip(core, b_to, core_to))
+
+    slots, gaps = [1], [jnp.float32(0.0)]
+
+    def prepare():
+        neigh_copy.wait()
+        tile = core * half + place
+        for n in (1, 2):
+            other = neigh[n, tile]
+            live = other >= 0
+            safe = jnp.where(live, other, tile)
+            away = jnp.where(lax.div(safe, half) == core, 0, 3)
+            slots.append(jnp.clip(away + lax.rem(safe, GRID_W) - x + 1, 0, 5))
+            gaps.append(jnp.where(live, jnp.float32(0.0), jnp.float32(1e30)))
 
     scale = 1.0 / math.sqrt(HD)
     rate = scale * math.log2(math.e)
-
-    neigh_copy.wait()
-    tile = core * half + place
-    slots, gaps = [1], [jnp.float32(0.0)]
-    for n in (1, 2):
-        other = neigh[n, tile]
-        live = other >= 0
-        safe = jnp.where(live, other, tile)
-        away = jnp.where(lax.div(safe, half) == core, 0, 3)
-        slots.append(jnp.clip(away + lax.rem(safe, GRID_W) - x + 1, 0, 5))
-        gaps.append(jnp.where(live, jnp.float32(0.0), jnp.float32(1e30)))
 
     def attend(j):
         drain(kw[j], sin_recv.at[j])
@@ -213,6 +216,7 @@
     sides, middles = (0, 1), (2, 3)
     gather(0, sides)
     gather(0, middles)
+    prepare()
     arrive(0, sides)
     gather(1, sides)
     spread(0)
@@ -251,12 +255,15 @@
         drain(kw[j], sin_send.at[j])
         drain(sib_send[j], sp_send.at[j])
         drain(x_send[j], xp_send.at[j])
-        drain(kw[j].at[0:3], out_send.at[j])
 
         @pl.when(jnp.logical_not(home))
         def _():
             drain(kw[j].at[0], zin_own.at[j])
-            drain(kw[j].at[0], out_own.at[j])
+            drain(kw[j].at[0:4], out_send.at[j])
+
+        @pl.when(home)
+        def _():
+            drain(kw[j].at[0:3], out_send.at[j])
 
     for n in range(4):
         drain(outs[n], out_recv.at[n])
@@ -283,27 +290,27 @@
         scratch += [pltpu.VMEM(shape, dtype)] * heads
     scratch += [dma((heads, 4)), dma((heads,)), dma((heads,)), dma((heads, 2)), dma((heads,))]
     scratch += [dma((heads,)), dma((heads,)), dma((heads,)), dma((heads,)), dma((heads, 2))]
-    scratch += [dma((heads,)), dma((4,)), dma((heads,)), dma((heads,))]
+    scratch += [dma((heads,)), dma((4,)), dma((heads,))]
     scratch += [pltpu.SMEM(neighbours.shape[::-1], jnp.int32), dma]
     anywhere = pl.BlockSpec(memory_space=pl.ANY)
     hbm = pl.BlockSpec(memory_space=pltpu.HBM)
     work = heads * TILE * 3 * TILE
-    shapes = pltpu.VMEM((4, rows, feat), low)
+    result = pltpu.VMEM((4, rows, feat), low)
     sources = (neighbours.T, key_rows, value_rows, query_rows, cotangent)
     landed = pl.pallas_call(
-            functools.partial(kernel, heads),
-            out_shape=shapes,
-            in_specs=[hbm] * 5,
-            out_specs=anywhere,
-            scratch_shapes=scratch,
-            compiler_params=pltpu.CompilerParams(
-                collective_id=0, has_side_effects=True, vmem_limit_bytes=VMEM
-            ),
-            cost_estimate=pl.CostEstimate(
-                flops=work * HD * 12, bytes_accessed=rows * feat * 16, transcendentals=work
-            ),
-            name="tile_attention",
-        )(*(pltpu.with_memory_space_constraint(source, pltpu.HBM) for source in sources))
+        functools.partial(kernel, heads),
+        out_shape=result,
+        in_specs=[hbm] * 5,
+        out_specs=anywhere,
+        scratch_shapes=scratch,
+        compiler_params=pltpu.CompilerParams(
+            collective_id=0, has_side_effects=True, vmem_limit_bytes=VMEM
+        ),
+        cost_estimate=pl.CostEstimate(
+            flops=work * HD * 12, bytes_accessed=rows * feat * 16, transcendentals=work
+        ),
+        name="tile_attention",
+    )(*(pltpu.with_memory_space_constraint(source, pltpu.HBM) for source in sources))
     return landed[0], landed[1], landed[2], landed[3]
 
 

time: 67.4 us -> 67.3 us (level)
  no operation moved by 1% of the time
where the time goes in v4:
time: 67.3 us; the launch traced here: 66.8 us
  Pallas kernels  65.1 us (97%)
  local copies, waits for them, and re-layouts  1.03 us (2%)
    pallas_call x1, Pallas kernels, on_device(): pl.pallas_call(functools.partial(kernel, heads), out_shape=result, in_spe...  65.1 us

profile of v4, /device:TPU:56, one launch (start us, length us, event | category | flops | bytes accessed | tf_op | source)
XLA Modules:
  0.0 66.8 jit_solution(986209619284572552)
XLA Ops:
  0.6 65.1 %tile_attention.1 = bf16[4,96,1536]{2,1,0:T(8,128)(2,1)S(1)} custom-call(s32[3,128]{1,0:T(4,128)} %bitcast.9, bf16[96,1536]{1,0:T(8,128)(2,1)} %refs_0_.1, bf16[96,1536]{1,0:T(8,128)(2,1)} %refs_1_.1, bf16[96,1536]{1,0:T(8,128)(2,1)} %refs_2_.1, bf16[96,1536]{1,0:T(8,128)(2,1)} %refs_3_.1), custom_call_target="tpu_custom_call" | custom-call | flops 2038431744 | bytes 2359296 | tf_op jit(solution)/shard_map/tile_attention/pallas_call | solution.py:300
  65.8 1.0 %slice_bitcast_fusion = (bf16[96,1536]{1,0:T(8,128)(2,1)}, bf16[96,1536]{1,0:T(8,128)(2,1)}, bf16[96,1536]{1,0:T(8,128)(2,1)}, bf16[96,1536]{1,0:T(8,128)(2,1)}) fusion(bf16[4,96,1536]{2,1,0:T(8,128)(2,1)S(1)} %tile_attention.1), kind=kLoop, calls=%fused_computation | loop fusion | bytes 2359296 | tf_op jit(solution)/shard_map/squeeze | solution.py:314

commit v5 on v4

--- a/solution.py
+++ b/solution.py
@@ -242,12 +242,20 @@
     give(1)
     arrive(2, middles)
     attend(2)
-    release(2, sides)
+
+    @pl.when(core == 0)
+    def _():
+        release(2, sides)
+
     give(2)
     finish(1)
     release(1, middles)
     finish(2)
     release(2, middles)
+
+    @pl.when(core == 1)
+    def _():
+        release(2, sides)
 
     for j in range(heads):
         drain(kw[j].at[0:3], zin_send.at[j])

time: 67.3 us -> 67 us (level)
  no operation moved by 1% of the time
where the time goes in v5:
time: 67 us; the launch traced here: 66.4 us
  Pallas kernels  64.7 us (97%)
  local copies, waits for them, and re-layouts  1.03 us (2%)
    pallas_call x1, Pallas kernels, on_device(): pl.pallas_call(functools.partial(kernel, heads), out_shape=result, in_spe...  64.7 us

profile of v5, /device:TPU:56, one launch (start us, length us, event | category | flops | bytes accessed | tf_op | source)
XLA Modules:
  0.0 66.4 jit_solution(9340607879702853779)
XLA Ops:
  0.6 64.7 %tile_attention.1 = bf16[4,96,1536]{2,1,0:T(8,128)(2,1)S(1)} custom-call(s32[3,128]{1,0:T(4,128)} %bitcast.9, bf16[96,1536]{1,0:T(8,128)(2,1)} %refs_0_.1, bf16[96,1536]{1,0:T(8,128)(2,1)} %refs_1_.1, bf16[96,1536]{1,0:T(8,128)(2,1)} %refs_2_.1, bf16[96,1536]{1,0:T(8,128)(2,1)} %refs_3_.1), custom_call_target="tpu_custom_call" | custom-call | flops 2038431744 | bytes 2359296 | tf_op jit(solution)/shard_map/tile_attention/pallas_call | solution.py:308
  65.4 1.0 %slice_bitcast_fusion = (bf16[96,1536]{1,0:T(8,128)(2,1)}, bf16[96,1536]{1,0:T(8,128)(2,1)}, bf16[96,1536]{1,0:T(8,128)(2,1)}, bf16[96,1536]{1,0:T(8,128)(2,1)}) fusion(bf16[4,96,1536]{2,1,0:T(8,128)(2,1)S(1)} %tile_attention.1), kind=kLoop, calls=%fused_computation | loop fusion | bytes 2359296 | tf_op jit(solution)/shard_map/squeeze | solution.py:322
